TPU v7x, 256 devices: a whole 4x4x8 slice. The times are simulated.
256 devices in a mesh: pair: 64 (over z_lo, x, y, core), chol: 4 (over z_hi).
Axes of the slice: x: 4, y: 4, z: 8 (z_hi: 4, z_lo: 2; z = z_hi * 2 + z_lo), core: 2. Of those that a mesh axis runs over, the one named last changes fastest.
Arguments:
- chol_ov: float32 [2048, 64, 768], P('chol', 'pair'), may hold values from -0.5 to 0.5
- chol_oo: float32 [2048, 64, 64], P('chol', 'pair'), may hold values from -0.5 to 0.5
- amplitudes: float32 [2, 64, 768], P(None, 'pair'), may hold values from -0.6 to 0.6
- eps_occ: float32 [64], P('pair'), may hold values from -2.5 to -0.4
- eps_vir: float32 [768], replicated, may hold values from 0.3 to 3
- fock: float32 [64, 768], P('pair'), may hold values from -0.3 to 0.3
Outputs:
- omega: float32 [2, 2, 768], replicated
All inputs are finite; a program needn't handle non-finite values.
Results may differ from a plain program's by a relative error of at most 0.00011.
Values sent between devices are 32-bit elements; how exact they have to be, the bound alone decides.
A program may use at most 64 MiB of HBM per device.

v0:
```python
import jax
import jax.numpy as jnp
from jax import lax
from jax.sharding import PartitionSpec as P

WIN = 2


STEP_TIME = 0.7


def broadcast(block, axis, owner):
    block = jnp.where(lax.axis_index(axis) == owner, block, jnp.zeros_like(block))
    return lax.psum(block, axis)


def dress(raw_ov, raw_oo, amps):
    count_q, count_n, count_v = raw_ov.shape
    flat = raw_oo.reshape(count_q * count_n, raw_oo.shape[2])
    real_part = raw_ov - jnp.dot(flat, amps[0], precision=lax.Precision.HIGHEST).reshape(
        count_q, count_n, count_v
    )
    imag_part = -jnp.dot(flat, amps[1], precision=lax.Precision.HIGHEST).reshape(
        count_q, count_n, count_v
    )
    return jnp.stack([real_part, imag_part])


def per_device(chol_ov, chol_oo, amplitudes, eps_occ, eps_vir, fock):
    hi = lax.Precision.HIGHEST
    amps = lax.all_gather(amplitudes, "pair", axis=1, tiled=True)
    dressed = dress(chol_ov, chol_oo, amps)
    count_n = chol_ov.shape[1]
    real_rows = []
    imag_rows = []
    for window in range(WIN):
        owner = window // count_n
        local = window % count_n
        left, e_left = (
            broadcast(dressed[:, :, local, :], "pair", owner),
            broadcast(eps_occ, "pair", owner),
        )
        g_real = jnp.einsum("qa,qnb->nab", left[0], dressed[0], precision=hi) - jnp.einsum(
            "qa,qnb->nab", left[1], dressed[1], precision=hi
        )
        g_imag = jnp.einsum("qa,qnb->nab", left[0], dressed[1], precision=hi) + jnp.einsum(
            "qa,qnb->nab", left[1], dressed[0], precision=hi
        )
        denom = eps_vir[None, :, None] + eps_vir[None, None, :] - e_left[0] - eps_occ[:, None, None]
        w_real = (1.0 - jnp.cos(STEP_TIME * denom)) / denom
        w_imag = jnp.sin(STEP_TIME * denom) / denom
        t_real = w_real * g_real - w_imag * g_imag
        t_imag = w_real * g_imag + w_imag * g_real
        o_real = 2.0 * jnp.einsum("nab,nb->a", t_real, fock, precision=hi) - jnp.einsum(
            "nba,nb->a", t_real, fock, precision=hi
        )
        o_imag = 2.0 * jnp.einsum("nab,nb->a", t_imag, fock, precision=hi) - jnp.einsum(
            "nba,nb->a", t_imag, fock, precision=hi
        )
        real_rows.append(o_real)
        imag_rows.append(o_imag)
    partial_terms = jnp.stack([jnp.stack(real_rows), jnp.stack(imag_rows)])
    return lax.psum(partial_terms, ("pair", "chol"))


def solution(mesh):
    return jax.shard_map(
        per_device,
        mesh=mesh,
        in_specs=(
            P("chol", "pair", None),
            P("chol", "pair", None),
            P(None, "pair", None),
            P("pair"),
            P(),
            P("pair", None),
        ),
        out_specs=P(),
        check_vma=False,
    )
```

profile of v0, /device:TPU:1, one launch (start us, length us, event | category | flops | bytes accessed | tf_op | source)
XLA Modules:
  0.0 889.4 jit_solution(5122807655321371239)
XLA Ops:
  6.5 0.0 copy-start
  6.5 0.0 all-reduce.4.cloned.1.call-start
  6.5 0.0 copy-start.3
  6.5 0.8 copy.8
  7.4 85.0 %all_gather.3 = f32[2,64,768]{2,0,1:T(2,128)S(1)} all-gather(f32[2,1,768]{2,0,1:T(2,128)S(1)} %copy.8), channel_id=1, replica_groups=mesh['pair'=64,'chol'=4] {'pair'}, dimensions={1}, use_global_device_ids=true | all-gather | bytes 399360 | tf_op jit(solution)/shard_map/all_gather | solution.py:31
  92.4 0.3 fusion.86
  92.7 0.0 copy-done
  92.7 1.4 convolution_negate_fusion
  94.2 0.0 copy-done.3
  94.2 1.5 bitcast_subtract_fusion
  95.6 3.1 select_bitcast_fusion.1
  98.8 0.0 all-reduce.4.cloned.1.call-update
  99.5 139.8 %all-reduce = (f32[]{:T(128)}, f32[]{:T(128)}) all-reduce(f32[]{:T(128)} %bitcast.17, f32[]{:T(128)} %bitcast.1), channel_id=1, replica_groups=mesh['pair'=64,'chol'=4] {'pair'}, use_global_device_ids=true, to_apply=%region_2.3 | all-reduce | flops 2 | bytes 16 | tf_op jit(solution)/shard_map/psum | solution.py:14
  239.2 427.1 %all-reduce.4.cloned.1.call-done = (f32[2,512,768]{2,1,0:T(8,128)}, f32[2,512,768]{2,1,0:T(8,128)}) async-done(((f32[2,512,768]{2,1,0:T(8,128)}, f32[2,512,768]{2,1,0:T(8,128)}), (f32[2,512,768]{2,1,0:T(8,128)}, f32[2,512,768]{2,1,0:T(8,128)})) %all-reduce.4.cloned.1.call-update) | async-done | bytes 6291472 | tf_op jit(solution)/shard_map/psum | solution.py:14
  666.3 0.0 copy-start.2
  666.3 6.0 fusion.35
  672.3 0.0 copy-done.2
  672.3 0.0 copy-start.1
  672.3 4.4 fusion.29
  676.8 0.0 copy-done.1
  676.8 5.0 fusion.34
  681.8 4.4 fusion.32
  686.2 4.5 convolution_add_fusion
  690.7 0.0 copy-start.4
  690.8 0.0 copy-start.5
  690.8 4.7 convolution_subtract_fusion
  695.5 0.0 copy-done.4
  695.5 0.0 copy-done.5
  695.5 12.4 %convolution_reduce_fusion = f32[768]{0:T(1024)S(1)} fusion(f32[768,768]{1,0:T(8,128)S(1)} %convolution_subtract_fusion, f32[768,768]{1,0:T(8,128)S(1)} %convolution_add_fusion, f32[]{:T(128)} %bitcast.179, f32[]{:T(128)} %get-tuple-element.5, f32[768]{0:T(1024)S(1)} %copy-done.4, f32[1,768]{1,0:T(1,128)S(1)} %copy-done.5), kind=kOutput, calls=%fused_computation.63 | convolution fusion | flops 12976128 | bytes 4727816 | tf_op jit(solution)/shard_map/nba,nb->a/dot_general | solution.py:54
  707.9 12.6 %fusion.45 = f32[768]{0:T(1024)S(1)} fusion(f32[768,768]{1,0:T(8,128)S(1)} %convolution_subtract_fusion, f32[768,768]{1,0:T(8,128)S(1)} %convolution_add_fusion, f32[]{:T(128)} %bitcast.177, f32[]{:T(128)} %get-tuple-element.5, f32[768]{0:T(1024)S(1)} %copy-done.4, f32[1,768]{1,0:T(1,128)S(1)} %copy-done.5), kind=kOutput, calls=%fused_computation.62 | convolution fusion | flops 12976128 | bytes 4727816 | tf_op jit(solution)/shard_map/nba,nb->a/dot_general | solution.py:57
  720.5 12.2 %fusion.42 = f32[768]{0:T(1024)S(1)} fusion(f32[768,768]{1,0:T(8,128)S(1)} %convolution_subtract_fusion, f32[768,768]{1,0:T(8,128)S(1)} %convolution_add_fusion, f32[]{:T(128)} %bitcast.172, f32[]{:T(128)} %get-tuple-element.5, f32[768]{0:T(1024)S(1)} %copy-done.4, f32[1,768]{1,0:T(1,128)S(1)} %copy-done.5), kind=kOutput, calls=%fused_computation.61 | convolution fusion | flops 12976128 | bytes 4727816 | tf_op jit(solution)/shard_map/nab,nb->a/dot_general | solution.py:57
  732.7 12.3 %convolution_reduce_fusion.1 = f32[768]{0:T(1024)S(1)} fusion(f32[768,768]{1,0:T(8,128)S(1)} %convolution_subtract_fusion, f32[768,768]{1,0:T(8,128)S(1)} %convolution_add_fusion, f32[]{:T(128)} %bitcast.173, f32[]{:T(128)} %get-tuple-element.5, f32[768]{0:T(1024)S(1)} %copy-done.4, f32[1,768]{1,0:T(1,128)S(1)} %copy-done.5), kind=kOutput, calls=%fused_computation.64 | convolution fusion | flops 12976128 | bytes 4727816 | tf_op jit(solution)/shard_map/nab,nb->a/dot_general | solution.py:54
  745.1 4.5 convolution_add_fusion.1
  749.6 4.5 convolution_subtract_fusion.1
  754.2 12.4 %convolution_reduce_fusion.2 = f32[768]{0:T(1024)S(1)} fusion(f32[768,768]{1,0:T(8,128)S(1)} %convolution_subtract_fusion.1, f32[768,768]{1,0:T(8,128)S(1)} %convolution_add_fusion.1, f32[]{:T(128)} %bitcast.178, f32[]{:T(128)} %get-tuple-element.6, f32[768]{0:T(1024)S(1)} %copy-done.4, f32[1,768]{1,0:T(1,128)S(1)} %copy-done.5), kind=kOutput, calls=%fused_computation.65 | convolution fusion | flops 12976128 | bytes 4727816 | tf_op jit(solution)/shard_map/nba,nb->a/dot_general | solution.py:54
  766.6 12.6 %fusion.39 = f32[768]{0:T(1024)S(1)} fusion(f32[768,768]{1,0:T(8,128)S(1)} %convolution_subtract_fusion.1, f32[768,768]{1,0:T(8,128)S(1)} %convolution_add_fusion.1, f32[]{:T(128)} %bitcast.176, f32[]{:T(128)} %get-tuple-element.6, f32[768]{0:T(1024)S(1)} %copy-done.4, f32[1,768]{1,0:T(1,128)S(1)} %copy-done.5), kind=kOutput, calls=%fused_computation.60 | convolution fusion | flops 12976128 | bytes 4727816 | tf_op jit(solution)/shard_map/nba,nb->a/dot_general | solution.py:57
  779.3 12.2 %fusion.36 = f32[768]{0:T(1024)S(1)} fusion(f32[768,768]{1,0:T(8,128)S(1)} %convolution_subtract_fusion.1, f32[768,768]{1,0:T(8,128)S(1)} %convolution_add_fusion.1, f32[]{:T(128)} %bitcast.175, f32[]{:T(128)} %get-tuple-element.6, f32[768]{0:T(1024)S(1)} %copy-done.4, f32[1,768]{1,0:T(1,128)S(1)} %copy-done.5), kind=kOutput, calls=%fused_computation.59 | convolution fusion | flops 12976128 | bytes 4727816 | tf_op jit(solution)/shard_map/nab,nb->a/dot_general | solution.py:57
  791.4 12.4 %convolution_reduce_fusion.3 = f32[768]{0:T(1024)S(1)} fusion(f32[768,768]{1,0:T(8,128)S(1)} %convolution_subtract_fusion.1, f32[768,768]{1,0:T(8,128)S(1)} %convolution_add_fusion.1, f32[]{:T(128)} %bitcast.174, f32[]{:T(128)} %get-tuple-element.6, f32[768]{0:T(1024)S(1)} %copy-done.4, f32[1,768]{1,0:T(1,128)S(1)} %copy-done.5), kind=kOutput, calls=%fused_computation.66 | convolution fusion | flops 12976128 | bytes 4727816 | tf_op jit(solution)/shard_map/nab,nb->a/dot_general | solution.py:54
  803.9 78.5 %psum.39 = f32[2,2,768]{2,1,0:T(2,128)} all-reduce(f32[2,2,768]{2,1,0:T(2,128)S(1)} %pad_maximum_fusion.1), channel_id=1, replica_groups=mesh['pair'=64,'chol'=4] {'pair','chol'}, use_global_device_ids=true, to_apply=%region_4.5 | all-reduce | flops 3072 | bytes 24576 | tf_op jit(solution)/shard_map/psum | solution.py:63
  (10 shorter events, 0.1 us)
Async XLA Ops:
  6.5 86.2 %copy-start = (f32[512,1,64]{0,2,1:T(8,128)S(1)}, f32[512,1,64]{0,2,1:T(8,128)}, u32[]{:S(2)}) copy-start(f32[512,1,64]{0,2,1:T(8,128)} %param.7) | copy-start | bytes 393220
  6.5 659.8 %all-reduce.4.cloned.1.call-start = ((), (), s32[]{:S(2)}) async-start(), calls=%async_computation | async-start | bytes 12582912 | tf_op jit(solution)/shard_map/psum | solution.py:14
  6.5 87.6 %copy-start.3 = (f32[512,1,768]{2,1,0:T(1,128)S(1)}, f32[512,1,768]{2,1,0:T(1,128)}, u32[]{:S(2)}) copy-start(f32[512,1,768]{2,1,0:T(1,128)} %param.6) | copy-start | bytes 4718596
  666.3 6.0 copy-start.2
  672.3 4.4 copy-start.1
  690.7 4.8 copy-start.4
  690.8 4.8 copy-start.5
Sparse Core Ops, SparseCore 0:
  98.9 567.3 all-reduce.3
where the time goes:
time: 893 us; the launch traced here: 889 us
  waiting for transfers between devices  427 us (48%)
  blocking collectives  303 us (34%)
  matrix products  140 us (16%)
  between operations  14.5 us (2%)
    psum x1, waiting for transfers between devices, broadcast(): return lax.psum(block, axis)  427 us
    psum x1, blocking collectives, broadcast(): return lax.psum(block, axis)  140 us
    all_gather x1, blocking collectives, per_device(): amps = lax.all_gather(amplitudes, 'pair', axis=1, tiled=True)  85 us
    psum x1, blocking collectives, per_device(): return lax.psum(partial_terms, ('pair', 'chol'))  78.5 us
    dot_general x2, matrix products, per_device(): jnp.einsum('nba,nb->a', t_imag, fock, precision=hi)  25.2 us
    dot_general x2, matrix products, per_device(): jnp.einsum('nba,nb->a', t_real, fock, precision=hi)  24.8 us
    dot_general x2, matrix products, per_device(): jnp.einsum('nab,nb->a', t_real, fock, precision=hi)  24.7 us
    dot_general x2, matrix products, per_device(): jnp.einsum('nab,nb->a', t_imag, fock, precision=hi)  24.3 us
  transfers between devices with their start and end apart: 1, of which 1 were waited for; matrix products, arithmetic and copies ran while one was open for 0% of the time, Pallas kernels for 0%

commit v1 on v0

v1 whole, which is shorter than its diff:
```python
import math

import jax
import jax.numpy as jnp
from jax import lax
from jax.experimental import pallas as pl
from jax.experimental.pallas import tpu as pltpu
from jax.sharding import PartitionSpec as P

WIN = 2
STEP_TIME = 0.7
HALF = STEP_TIME / 2
RANK = 8
VIR_LOW, VIR_HIGH = 0.3, 3.0
OCC_LOW, OCC_HIGH = -2.5, -0.4
PAIR, CHOL = 64, 4
SLOTS = PAIR // 2
PLANE = 16
LINE = 8
V, NQ, O = 768, 512, 64
ROW = 2 * V + 128
MESH = pl.DeviceIdType.MESH
F32 = jnp.float32
BF16 = jnp.bfloat16
NN = (((1,), (0,)), ((), ()))
NT = (((1,), (1,)), ((), ()))


def nodes_on(low, high):
    mid, half = (low + high) / 2, (high - low) / 2
    return [mid + half * math.cos((2 * m + 1) * math.pi / (2 * RANK)) for m in range(RANK)]


VIR_NODES = nodes_on(VIR_LOW, VIR_HIGH)
PAIR_NODES = nodes_on(VIR_LOW - OCC_HIGH, VIR_HIGH - OCC_LOW)
PAIR_MID = (VIR_LOW - OCC_HIGH + VIR_HIGH - OCC_LOW) / 2


def by_row(values, width):
    row = lax.broadcasted_iota(jnp.int32, (RANK, width), 0)
    out = jnp.full((RANK, width), values[0], F32)
    for m in range(1, RANK):
        out = jnp.where(row == m, F32(values[m]), out)
    return out


def basis(nodes, at):
    scale = []
    for m in range(RANK):
        den = 1.0
        for n in range(RANK):
            if n != m:
                den *= nodes[m] - nodes[n]
        scale.append(1.0 / den)
    width = at.shape[1]
    row = lax.broadcasted_iota(jnp.int32, (RANK, width), 0)
    out = by_row(scale, width)
    for n in range(RANK):
        out = out * jnp.where(row == n, F32(1.0), at - F32(nodes[n]))
    return out


def weight(denom):
    s, c = jnp.sin(HALF * denom), jnp.cos(HALF * denom)
    q = 2.0 * s / denom
    return q * s, q * c


def split(x):
    hi = x.astype(BF16)
    return hi, (x - hi.astype(F32)).astype(BF16)


def dot(a, b, dims):
    return lax.dot_general(a, b, dims, preferred_element_type=F32)


def dot3(a, b, dims):
    a_hi, a_lo = a
    b_hi, b_lo = b
    rows = a_hi.shape[0]
    both = dot(jnp.concatenate([a_hi, a_lo], axis=0), b_hi, dims)
    return both[:rows] + both[rows:] + dot(a_hi, b_lo, dims)


def kernel(
    ov, oo, amps, eocc, evir, fock, out,
    l_hi, l_lo, l_other, t_all, f_all, fm_hi, fm_lo, z_out, z_in, oo_out, oo_all,
    x_own, x_in, x_sum, x_all, x_fin, om, om_in, om_pl, om_ln, om_fin,
    t_snd, t_rcv, tp_snd, tp_rcv, f_snd, f_rcv, l_snd, l_rcv, z_snd, z_rcv,
    o_snd, o_rcv, oa_snd, oa_rcv, op_snd, op_rcv, xp_snd, xp_rcv, xr_snd, xr_rcv, xs_snd, xs_rcv,
    r1_snd, r1_rcv, r2_snd, r2_rcv, r3_snd, r3_rcv, r4_snd, r4_rcv,
):
    p, c = lax.axis_index("pair"), lax.axis_index("chol")
    core = lax.rem(p, 2)
    slot = p // 2
    peer = p + 1 - 2 * core
    plane = lax.rem(slot, PLANE)
    z_lo = p // (PAIR // 2)
    line = 2 * c + z_lo

    def copy(src, dst, snd, rcv, pair, chol):
        return pltpu.make_async_remote_copy(
            src_ref=src, dst_ref=dst, send_sem=snd, recv_sem=rcv,
            device_id=(pair, chol), device_id_type=MESH,
        )

    def local(ref, sem):
        return pltpu.make_async_copy(ref, ref, sem)

    def mate(k):
        return lax.rem(p + 2 * k, PAIR)

    def line_mate(k):
        z = lax.rem(line + k, LINE)
        return lax.rem(p, PAIR // 2) + (PAIR // 2) * lax.rem(z, 2), z // 2

    barrier = pltpu.get_barrier_semaphore()
    pl.semaphore_signal(barrier, inc=1, device_id=(peer, c), device_id_type=MESH)

    @pl.loop(1, SLOTS)
    def _(k):
        pl.semaphore_signal(barrier, inc=1, device_id=(mate(k), c), device_id_type=MESH)

    for k in range(1, LINE):
        @pl.when(lax.rem(line + k, LINE) // 2 != c)
        def _(k=k):
            pair, chol = line_mate(k)
            pl.semaphore_signal(barrier, inc=1, device_id=(pair, chol), device_id_type=MESH)

    e_vir = evir[...]
    e_own = eocc[...]
    f_row = fock[...]
    t_all[slot, core, :, 0:V] = amps[0:1, :]
    t_all[slot, core, :, V:2 * V] = amps[1:2, :]
    t_all[slot, core, :, 2 * V:ROW] = jnp.broadcast_to(e_own, (1, 128))

    @pl.when(slot == 0)
    def _():
        oo_t = jnp.transpose(oo[...])
        for k in range(SLOTS):
            oo_out[k] = oo_t[8 * (k // 4):8 * (k // 4) + 8, 128 * (k % 4):128 * (k % 4) + 128]

    poly = basis(VIR_NODES, jnp.broadcast_to(e_vir, (RANK, V)))
    gap = jnp.broadcast_to(e_vir - e_own, (RANK, V))
    turn = HALF * (gap - PAIR_MID)
    pair_poly = basis(PAIR_NODES, gap) * f_row
    f_vir = poly * f_row
    f_pair = jnp.concatenate([pair_poly * jnp.cos(turn), -pair_poly * jnp.sin(turn)], axis=0)
    hi, lo = split(ov[...])
    l_hi[...] = hi
    l_lo[...] = lo

    pl.semaphore_wait(barrier, 1 + (SLOTS - 1) + (LINE - 2))

    fock_copy = copy(fock, f_all.at[slot], f_snd, f_rcv, core, c)

    @pl.when(slot != 0)
    def _():
        fock_copy.start()

    slab_copy = copy(ov, l_other, l_snd, l_rcv, peer, c)

    @pl.when(slot == 0)
    def _():
        slab_copy.start()

        @pl.loop(1, SLOTS)
        def _(k):
            copy(oo_out.at[k], oo_all.at[core, pl.ds(pl.multiple_of(8 * (k // 4), 8), 8), pl.ds(pl.multiple_of(128 * lax.rem(k, 4), 128), 128)],
                 o_snd, o_rcv, 2 * k + core, c).start()

        oo_all[core, 0:8, 0:128] = oo_out[0]
        f_all[0] = fock[...]

    @pl.loop(1, SLOTS)
    def _(k):
        row = t_all.at[slot, core]
        copy(row, row, t_snd, t_rcv, mate(k), c).start()

    oo_mine = oo_all.at[core, pl.ds(pl.multiple_of(8 * (slot // 4), 8), 8), pl.ds(pl.multiple_of(128 * lax.rem(slot, 4), 128), 128)]

    def pass_on():
        @pl.loop(1, SLOTS)
        def _(k):
            copy(oo_mine, oo_mine, oa_snd, oa_rcv, mate(k), c).start()

    @pl.when(slot == 0)
    def _():
        pass_on()
        local(f_all.at[pl.ds(1, SLOTS - 1)], f_rcv).wait()
        for k in range(0, SLOTS, 2):
            pairs = jnp.concatenate([poly * f_all[k], poly * f_all[k + 1]], axis=0)
            hi, lo = split(pairs)
            fm_hi[8 * k:8 * k + 16, :] = hi
            fm_lo[8 * k:8 * k + 16, :] = lo

        def project(window, b_hi, b_lo):
            z = dot3((fm_hi[...], fm_lo[...]), (b_hi, b_lo), NT)
            for k in range(SLOTS):
                z_out[window, k] = z[8 * k:8 * k + 8, :]

            @pl.loop(1, SLOTS)
            def _(k):
                copy(z_out.at[window, k], z_in.at[window], z_snd.at[window], z_rcv.at[window], 2 * k + core, c).start()

            z_in[window] = z_out[window, 0]

        project(core, l_hi[...], l_lo[...])
        slab_copy.wait_recv()
        hi, lo = split(l_other[...])
        project(1 - core, hi, lo)

    @pl.when(slot != 0)
    def _():
        local(oo_mine, o_rcv).wait()
        pass_on()

    local(t_all.at[pl.ds(0, SLOTS - 1), core], t_rcv).wait()
    rows = t_all.at[:, core]
    t_swap = copy(rows, rows, tp_snd, tp_rcv, peer, c)
    t_swap.start()
    x_left = dot3(split(f_pair), (l_hi[...], l_lo[...]), NT)
    other_rows = t_all.at[:, 1 - core]
    copy(other_rows, other_rows, tp_snd, tp_rcv, peer, c).wait_recv()
    t_re = split(t_all[:, :, 0, 0:V].reshape(O, V))
    t_im = split(t_all[:, :, 0, V:2 * V].reshape(O, V))
    lhs = split(jnp.concatenate([f_vir, f_pair], axis=0))
    tf_re, tf_im = dot3(lhs, t_re, NT), dot3(lhs, t_im, NT)
    oo_own = split(oo[...])
    tx = jnp.concatenate([tf_re[8:16] - tf_im[16:24], tf_im[8:16] + tf_re[16:24]], axis=0)
    x_terms = x_left - dot3(split(tx), oo_own, NT)
    x_own[0] = x_terms[0:8]
    x_own[1] = x_terms[8:16]
    x_swap = copy(x_own.at[1 - core], x_in, xp_snd, xp_rcv, peer, c)
    x_swap.start()
    x_swap.wait_recv()
    x_sum[...] = x_own[core] + x_in[...]
    x_copy = copy(x_sum, x_all.at[slot], xr_snd, xr_rcv, core, c)

    @pl.when(slot != 0)
    def _():
        x_copy.start()

    local(oo_out.at[pl.ds(0, SLOTS - 1)], oa_rcv).wait()
    oo_swap = copy(oo_all.at[core], oo_all.at[core], op_snd, op_rcv, peer, c)
    oo_swap.start()
    copy(oo_all.at[1 - core], oo_all.at[1 - core], op_snd, op_rcv, peer, c).wait_recv()
    tz = split(jnp.concatenate([tf_re[0:8], tf_im[0:8]], axis=0))
    dress = [dot3(tz, split(oo_all[i]), NN) for i in range(WIN)]

    def through(ct):
        ct = split(ct)
        lv = dot3(ct, (l_hi[...], l_lo[...]), NN)
        r = split(dot3(ct, oo_own, NN))
        rt_re, rt_im = dot3(r, t_re, NN), dot3(r, t_im, NN)
        parts = []
        for g in range(0, lv.shape[0], 16):
            re, im = slice(g, g + 8), slice(g + 8, g + 16)
            parts.append((
                lv[re] - (rt_re[re] - rt_im[im]),
                lv[im] - (rt_im[re] + rt_re[im]),
            ))
        return parts

    def fold(w_re, w_im, v_re, v_im):
        re = jnp.sum(w_re * v_re - w_im * v_im, axis=0, keepdims=True)
        im = jnp.sum(w_re * v_im + w_im * v_re, axis=0, keepdims=True)
        return re, im

    e_win = [t_all[0, i, :, 2 * V:2 * V + 1] for i in range(WIN)]

    @pl.when(slot != 0)
    def _():
        for i in range(WIN):
            local(z_in.at[i], z_rcv.at[i]).wait()

    cols = []
    for i in range(WIN):
        cols += [z_in[i] - dress[i][0:8], -dress[i][8:16]]
    vir_rows = by_row(VIR_NODES, V)
    for i, (v_re, v_im) in enumerate(through(jnp.concatenate(cols, axis=0))):
        w_re, w_im = weight(e_vir + vir_rows - (e_win[i] + e_own))
        re, im = fold(w_re, w_im, v_re, v_im)
        om[i, :, 0:V] = -re
        om[i, :, V:2 * V] = -im

    @pl.when(slot == 0)
    def _():
        x_all[0] = x_sum[...]
        local(x_all.at[pl.ds(1, SLOTS - 1)], xr_rcv).wait()
        total = x_all[0]
        for k in range(1, SLOTS):
            total = total + x_all[k]
        x_fin[core] = total
        swap = copy(x_fin.at[core], x_fin.at[core], xs_snd, xs_rcv, peer, c)
        swap.start()
        copy(x_fin.at[1 - core], x_fin.at[1 - core], xs_snd, xs_rcv, peer, c).wait_recv()
        (v_re, v_im), = through(jnp.concatenate([x_fin[0], x_fin[1]], axis=0))
        w_re, w_im = weight(e_vir + by_row(PAIR_NODES, V) - e_own)
        turns = [HALF * (g - PAIR_MID) for g in PAIR_NODES]
        t_cos = by_row([math.cos(g) for g in turns], V)
        t_sin = by_row([math.sin(g) for g in turns], V)
        re, im = fold(w_re * t_cos - w_im * t_sin, w_re * t_sin + w_im * t_cos, v_re, v_im)
        om[core, :, 0:V] += 2.0 * re
        om[core, :, V:2 * V] += 2.0 * im
        swap.wait_send()

    first = copy(om.at[1 - core], om_in, r1_snd, r1_rcv, peer, c)
    first.start()
    first.wait_recv()
    om_pl[plane] = om[core] + om_in[...]

    @pl.loop(1, PLANE)
    def _(k):
        to = (PAIR // 2) * z_lo + lax.rem(lax.rem(p, PAIR // 2) + 2 * k, PAIR // 2)
        copy(om_pl.at[plane], om_pl.at[plane], r2_snd, r2_rcv, to, c).start()

    local(om_pl.at[pl.ds(0, PLANE - 1)], r2_rcv).wait()
    total = om_pl[0]
    for k in range(1, PLANE):
        total = total + om_pl[k]
    om_ln[line] = total
    for k in range(1, LINE):
        pair, chol = line_mate(k)
        copy(om_ln.at[line], om_ln.at[line], r3_snd, r3_rcv, pair, chol).start()
    local(om_ln.at[pl.ds(0, LINE - 1)], r3_rcv).wait()
    total = om_ln[0]
    for k in range(1, LINE):
        total = total + om_ln[k]
    om_fin[core] = total
    last = copy(om_fin.at[core], om_fin.at[core], r4_snd, r4_rcv, peer, c)
    last.start()
    copy(om_fin.at[1 - core], om_fin.at[1 - core], r4_snd, r4_rcv, peer, c).wait_recv()
    for i in range(WIN):
        for r in range(2):
            out[r, i:i + 1, :] = om_fin[i, :, r * V:(r + 1) * V]

    last.wait_send()
    local(om_ln.at[pl.ds(0, LINE - 1)], r3_snd).wait()
    local(om_pl.at[pl.ds(0, PLANE - 1)], r2_snd).wait()
    first.wait_send()
    oo_swap.wait_send()
    x_swap.wait_send()
    t_swap.wait_send()
    local(oo_out.at[pl.ds(0, SLOTS - 1)], oa_snd).wait()
    local(t_all.at[pl.ds(0, SLOTS - 1), core], t_snd).wait()

    @pl.when(slot != 0)
    def _():
        fock_copy.wait_send()
        x_copy.wait_send()

    @pl.when(slot == 0)
    def _():
        slab_copy.wait_send()
        local(oo_out.at[pl.ds(0, SLOTS - 1)], o_snd).wait()
        for i in range(WIN):
            local(z_out.at[i, pl.ds(0, SLOTS - 1)], z_snd.at[i]).wait()


def per_device(chol_ov, chol_oo, amplitudes, eps_occ, eps_vir, fock):
    vmem = pl.BlockSpec(memory_space=pltpu.VMEM)
    dma = pltpu.SemaphoreType.DMA
    scratch = [
        pltpu.VMEM((NQ, V), BF16), pltpu.VMEM((NQ, V), BF16), pltpu.VMEM((NQ, V), F32),
        pltpu.VMEM((SLOTS, 2, 1, ROW), F32), pltpu.VMEM((SLOTS, 1, V), F32),
        pltpu.VMEM((SLOTS * RANK, V), BF16), pltpu.VMEM((SLOTS * RANK, V), BF16),
        pltpu.VMEM((WIN, SLOTS, RANK, NQ), F32), pltpu.VMEM((WIN, RANK, NQ), F32),
        pltpu.VMEM((SLOTS, 8, 128), F32), pltpu.VMEM((WIN, O, NQ), F32),
        pltpu.VMEM((2, RANK, NQ), F32), pltpu.VMEM((RANK, NQ), F32), pltpu.VMEM((RANK, NQ), F32),
        pltpu.VMEM((SLOTS, RANK, NQ), F32), pltpu.VMEM((2, RANK, NQ), F32),
        pltpu.VMEM((WIN, 1, 2 * V), F32), pltpu.VMEM((1, 2 * V), F32),
        pltpu.VMEM((PLANE, 1, 2 * V), F32), pltpu.VMEM((LINE, 1, 2 * V), F32),
        pltpu.VMEM((WIN, 1, 2 * V), F32),
    ]
    sems = [dma] * 8 + [dma((WIN,))] * 2 + [dma] * 20
    return pl.pallas_call(
        kernel,
        out_shape=jax.ShapeDtypeStruct((2, WIN, V), F32),
        in_specs=[vmem] * 6,
        out_specs=vmem,
        scratch_shapes=scratch + sems,
        compiler_params=pltpu.CompilerParams(
            collective_id=0, has_side_effects=True, vmem_limit_bytes=40 * 2**20
        ),
    )(
        chol_ov.reshape(NQ, V), chol_oo.reshape(NQ, O), amplitudes.reshape(2, V),
        eps_occ.reshape(1, 1), eps_vir.reshape(1, V), fock.reshape(1, V),
    )


def solution(mesh):
    return jax.shard_map(
        per_device,
        mesh=mesh,
        in_specs=(
            P("chol", "pair", None),
            P("chol", "pair", None),
            P(None, "pair", None),
            P("pair"),
            P(),
            P("pair", None),
        ),
        out_specs=P(),
        check_vma=False,
    )
```

time: 893 us -> 47.8 us (0.05)
  waiting for transfers between devices: 427 us -> 0 us
  blocking collectives: 303 us -> 0 us
  matrix products: 140 us -> 0 us
  Pallas kernels: 0 us -> 42.4 us
  between operations: 14.5 us -> 0.69 us
    psum x1 -> x0, waiting for transfers between devices: 427 us -> none  [broadcast(): return lax.psum(block, axis)]
    psum x2 -> x0, blocking collectives: 218 us -> none  [the longest x1 140 us: broadcast(): return lax.psum(block, axis)]
    dot_general x18 -> x0, matrix products: 140 us -> none  [the longest x2 25.2 us: per_device(): jnp.einsum('nba,nb->a', t_imag, fock, precision=hi)]
    all_gather x1 -> x0, blocking collectives: 85 us -> none  [per_device(): amps = lax.all_gather(amplitudes, 'pair', axis=1, tiled=True)]
    pallas_call x0 -> x1, Pallas kernels: none -> 42.4 us  [per_device(): pl.pallas_call(kernel, out_shape=jax.ShapeDtypeStruct((2, WIN, V), F32),...]
  transfers between devices with their start and end apart: 1 -> 0, of which waited for: 1 -> 0; matrix products, arithmetic and copies ran while one was open for 0% -> 0% of each run, Pallas kernels for 0% -> 0%
where the time goes in v1:
time: 47.8 us; the launch traced here: 47.6 us
  Pallas kernels  42.4 us (89%)
  local copies, waits for them, and re-layouts  4.54 us (9%)
  between operations  0.69 us (1%)
    pallas_call x1, Pallas kernels, per_device(): pl.pallas_call(kernel, out_shape=jax.ShapeDtypeStruct((2, WIN, V), F32),...  42.4 us
    unnamed x6, local copies, waits for them, and re-layouts  3.85 us

profile of v1, /device:TPU:1, one launch (start us, length us, event | category | flops | bytes accessed | tf_op | source)
XLA Modules:
  0.0 47.6 jit_solution(7397738137391281064)
XLA Ops:
  0.7 0.7 %reshape.19.evir = f32[1,768]{1,0:T(1,128)S(1)} reshape(f32[768]{0:T(1024)} %param.10) | data formatting | bytes 6144 | tf_op jit(solution)/shard_map/reshape | solution.py:389
  1.3 0.7 %copy.13 = f32[2,1,768]{2,0,1:T(2,128)S(1)} copy(f32[2,1,768]{2,1,0:T(1,128)} %param.8) | data formatting | bytes 12288
  2.0 1.0 %copy.7 = f32[512,1,64]{2,0,1:T(8,128)S(1)} copy(f32[512,1,64]{0,2,1:T(8,128)} %param.7) | data formatting | bytes 262144 | tf_op args[1]
  3.1 0.0 copy-start
  3.1 1.5 %copy.12 = f32[512,1,768]{2,0,1:T(8,128)S(1)} copy(f32[512,1,768]{2,1,0:T(1,128)} %param.6) | data formatting | bytes 3145728
  4.6 0.0 copy-done
  4.6 42.4 %shard_map.64 = f32[2,2,768]{2,1,0:T(2,128)S(1)} custom-call(f32[512,768]{1,0:T(8,128)S(1)} %bitcast.9, f32[512,64]{1,0:T(8,128)S(1)} %bitcast.10, f32[2,768]{1,0:T(2,128)S(1)} %bitcast.11, f32[1,1]{1,0:T(1,128)} %bitcast.8.eocc, f32[1,768]{1,0:T(1,128)S(1)} %reshape.19.evir, f32[1,768]{1,0:T(1,128)S(1)} %copy-done), custom_call_target="tpu_custom_call" | custom-call | tf_op jit(solution)/shard_map/pallas_call | solution.py:378
  47.0 0.6 %copy.16 = f32[2,2,768]{2,1,0:T(2,128)} copy(f32[2,2,768]{2,1,0:T(2,128)S(1)} %shard_map.64) | data formatting | bytes 24576
Async XLA Ops:
  3.1 1.5 %copy-start = (f32[1,768]{1,0:T(1,128)S(1)}, f32[1,768]{1,0:T(1,128)}, u32[]{:S(2)}) copy-start(f32[1,768]{1,0:T(1,128)} %fock.1) | copy-start | bytes 9220

commit v2 on v1

v2 whole, which is shorter than its diff:
```python
import math

import jax
import jax.numpy as jnp
from jax import lax
from jax.experimental import pallas as pl
from jax.experimental.pallas import tpu as pltpu
from jax.sharding import PartitionSpec as P

WIN = 2
STEP_TIME = 0.7
HALF = STEP_TIME / 2
RANK = 8
VIR_LOW, VIR_HIGH = 0.3, 3.0
OCC_LOW, OCC_HIGH = -2.5, -0.4
PAIR, CHOL = 64, 4
SLOTS = PAIR // 2
PLANE = 16
LINE = 8
V, NQ, O = 768, 512, 64
LANES = 128
VB = V // LANES
QUARTERS = NQ // LANES
UNIT = LANES * VB
EPS_AT, SENT, MSG = 2 * VB, 2 * VB + 1, 16
MESH = pl.DeviceIdType.MESH
F32 = jnp.float32
BF16 = jnp.bfloat16
NN = (((1,), (0,)), ((), ()))
NT = (((1,), (1,)), ((), ()))


def nodes_on(low, high):
    mid, half = (low + high) / 2, (high - low) / 2
    return [mid + half * math.cos((2 * m + 1) * math.pi / (2 * RANK)) for m in range(RANK)]


VIR_NODES = nodes_on(VIR_LOW, VIR_HIGH)
PAIR_NODES = nodes_on(VIR_LOW - OCC_HIGH, VIR_HIGH - OCC_LOW)
PAIR_MID = (VIR_LOW - OCC_HIGH + VIR_HIGH - OCC_LOW) / 2


def by_row(values, width):
    row = lax.broadcasted_iota(jnp.int32, (RANK, width), 0)
    out = jnp.full((RANK, width), values[0], F32)
    for m in range(1, RANK):
        out = jnp.where(row == m, F32(values[m]), out)
    return out


def basis(nodes, at):
    scale = []
    for m in range(RANK):
        den = 1.0
        for n in range(RANK):
            if n != m:
                den *= nodes[m] - nodes[n]
        scale.append(1.0 / den)
    width = at.shape[1]
    row = lax.broadcasted_iota(jnp.int32, (RANK, width), 0)
    out = by_row(scale, width)
    for n in range(RANK):
        out = out * jnp.where(row == n, F32(1.0), at - F32(nodes[n]))
    return out


def weight(denom):
    s, c = jnp.sin(HALF * denom), jnp.cos(HALF * denom)
    q = 2.0 * s / denom
    return q * s, q * c


def fold(w, v):
    re = jnp.sum(w[0] * v[0] - w[1] * v[1], axis=0, keepdims=True)
    im = jnp.sum(w[0] * v[1] + w[1] * v[0], axis=0, keepdims=True)
    return re, im


def split(x):
    hi = x.astype(BF16)
    return hi, (x - hi.astype(F32)).astype(BF16)


def dot(a, b, dims):
    return lax.dot_general(a, b, dims, preferred_element_type=F32)


def dot3(a, b, dims):
    a_hi, a_lo = a
    b_hi, b_lo = b
    rows = a_hi.shape[0]
    both = dot(jnp.concatenate([a_hi, a_lo], axis=0), b_hi, dims)
    return both[:rows] + both[rows:] + dot(a_hi, b_lo, dims)


def far_first(v):
    return 2 + v - (v // 2) * (2 * v - 1)


def kernel(
    ov, oo, amps, eocc, evir, fock, out,
    raw, oo_in, amps_in, e_in, ev_in, f_in, in_sem,
    oo_q, oo_p, oo_hi, oo_lo, l_hi, l_lo, x_left, msg,
    f_rows, l_other, lx_hi, lx_lo, oo_g, fm_hi, fm_lo, rhs_hi, rhs_lo, z_out, z_in,
    x_out, x_in, x_sum, x_all, x_tot, om, om_in, om_pl, om_ln, om_fin,
    z_snd, z_rcv, l_snd, l_rcv, f_snd, f_rcv, x_snd, x_rcv, xs_snd, xs_rcv, t_snd, t_rcv, tp_snd, tp_rcv,
    oc_snd, oc_rcv, oa_snd, oa_rcv, op_snd, op_rcv, xp_snd, xp_rcv, r1_snd, r1_rcv, r2_snd, r2_rcv, r3_snd, r3_rcv, r4_snd, r4_rcv,
):
    p, c = lax.axis_index("pair"), lax.axis_index("chol")
    core = lax.rem(p, 2)
    slot = p // 2
    peer = p + 1 - 2 * core
    z_lo, x_at, y_at = slot // PLANE, lax.rem(slot // 4, 4), lax.rem(slot, 4)
    plane = lax.rem(slot, PLANE)
    line = 2 * c + z_lo

    def copy(src, dst, snd, rcv, pair, chol):
        return pltpu.make_async_remote_copy(
            src_ref=src, dst_ref=dst, send_sem=snd, recv_sem=rcv,
            device_id=(pair, chol), device_id_type=MESH,
        )

    def local(ref, sem):
        return pltpu.make_async_copy(ref, ref, sem)

    def mate(k):
        z = lax.rem(z_lo + 1 - k // PLANE, 2)
        x = lax.rem(x_at + far_first(lax.rem(k // 4, 4)), 4)
        y = lax.rem(y_at + far_first(lax.rem(k, 4)), 4)
        return z * PLANE + x * 4 + y

    def line_mate(k):
        z = lax.rem(line + k, LINE)
        return lax.rem(p, PAIR // 2) + (PAIR // 2) * lax.rem(z, 2), z // 2

    far_line = (4, 3, 5, 2, 6, 1, 7)
    owner = slot == 0

    inputs = [
        pltpu.make_async_copy(src, dst, in_sem.at[i])
        for i, (src, dst) in enumerate(
            ((amps, amps_in), (fock, f_in), (eocc, e_in), (evir, ev_in), (oo, oo_in), (ov, raw))
        )
    ]
    for cp in inputs:
        cp.start()

    barrier = pltpu.get_barrier_semaphore()

    def greet(pair, chol):
        pl.semaphore_signal(barrier, inc=1, device_id=(pair, chol), device_id_type=MESH)

    for k in far_line:
        @pl.when(lax.rem(line + k, LINE) // 2 != c)
        def _(k=k):
            greet(*line_mate(k))

    @pl.loop(0, SLOTS - 1)
    def _(k):
        greet(2 * mate(k) + core, c)

    greet(peer, c)

    for cp in inputs[:3]:
        cp.wait()
    e_own = e_in[0]
    rows = [amps_in[r, :, LANES * b:LANES * (b + 1)] for r in range(2) for b in range(VB)]
    rows += [jnp.full((MSG - 2 * VB, LANES), e_own, F32)]
    msg[slot] = jnp.concatenate(rows, axis=0)
    flat = msg.reshape(PAIR * MSG, LANES)

    inputs[3].wait()
    e_vir = ev_in[...].reshape(1, V)
    f_row = f_in[...]
    poly = basis(VIR_NODES, jnp.broadcast_to(e_vir, (RANK, V)))
    gap = jnp.broadcast_to(e_vir - e_own, (RANK, V))
    turn = HALF * (gap - PAIR_MID)
    pair_poly = basis(PAIR_NODES, gap) * f_row
    f_pair = jnp.concatenate([pair_poly * jnp.cos(turn), -pair_poly * jnp.sin(turn)], axis=0)
    f_all = split(jnp.concatenate([poly * f_row, f_pair], axis=0))
    f_pair = split(f_pair)

    inputs[4].wait()
    for q in range(QUARTERS):
        oo_q[O * q:O * (q + 1), :] = oo_in[:, LANES * q:LANES * (q + 1)]
    for q in range(QUARTERS):
        at = O * q
        oo_p[at:at + 32, :] = oo_q[pl.ds(at + core, 32, stride=2), :]
        oo_p[at + 32:at + 64, :] = oo_q[pl.ds(at + 1 - core, 32, stride=2), :]
        hi, lo = split(oo_p[at:at + O, :])
        oo_hi[:, LANES * q:LANES * (q + 1)] = hi
        oo_lo[:, LANES * q:LANES * (q + 1)] = lo

    inputs[5].wait()
    for b in range(VB):
        hi, lo = split(raw[pl.ds(b, NQ, stride=VB), :])
        l_hi[:, LANES * b:LANES * (b + 1)] = hi
        l_lo[:, LANES * b:LANES * (b + 1)] = lo
    x_left[...] = dot3(f_pair, (l_hi[...], l_lo[...]), NT)

    pl.semaphore_wait(
        barrier,
        1 + (SLOTS - 1) + (LINE - 2),
    )

    f_copy = copy(f_in, f_rows.at[slot], f_snd, f_rcv, core, c)
    l_copy = copy(raw, l_other, l_snd, l_rcv, peer, c)

    @pl.when(jnp.logical_not(owner))
    def _():
        f_copy.start()

    @pl.when(owner)
    def _():
        l_copy.start()
        f_rows[0] = f_in[...]

    @pl.loop(0, SLOTS - 1)
    def _(k):
        mine = msg.at[slot, pl.ds(0, SENT)]
        copy(mine, mine, t_snd, t_rcv, 2 * mate(k) + core, c).start()

    def chunk(ref, s):
        return ref.at[pl.ds(pl.multiple_of(O * lax.rem(s, 4) + 8 * (s // 4), 8), 8)]

    def pass_on():
        @pl.loop(0, SLOTS - 1)
        def _(k):
            mine = chunk(oo_own_w, slot)
            copy(mine, mine, oa_snd, oa_rcv, 2 * mate(k) + core, c).start()

    oo_own_w = oo_g.at[0]

    @pl.when(owner)
    def _():
        @pl.loop(0, SLOTS - 1)
        def _(k):
            to = mate(k)
            copy(chunk(oo_p, to), chunk(oo_own_w, to), oc_snd, oc_rcv, 2 * to + core, c).start()

        oo_g[0, 0:8, :] = oo_p[0:8, :]
        pass_on()

    half = MSG * SLOTS
    chunks_in = oo_p.at[pl.ds(0, 8 * (SLOTS - 1))]
    local(msg.at[pl.ds(0, SLOTS - 1), pl.ds(0, SENT)], t_rcv).wait()
    t_swap = copy(msg.at[pl.ds(0, SLOTS), pl.ds(0, SENT)], msg.at[pl.ds(SLOTS, SLOTS), pl.ds(0, SENT)],
                  tp_snd, tp_rcv, peer, c)
    t_swap.start()

    def take_amps(h):
        for r in range(2):
            for b in range(VB):
                hi, lo = split(flat[pl.ds(half * h + VB * r + b, SLOTS, stride=MSG), :])
                at = slice(O * r + SLOTS * h, O * r + SLOTS * (h + 1))
                rhs_hi[at, LANES * b:LANES * (b + 1)] = hi
                rhs_lo[at, LANES * b:LANES * (b + 1)] = lo

    @pl.when(jnp.logical_not(owner))
    def _():
        local(chunk(oo_own_w, slot), oc_rcv).wait()
        pass_on()

    def project(w, slab):
        z = dot3((fm_hi[...], fm_lo[...]), slab, NT)
        for s in range(SLOTS):
            z_out[w, s] = z[RANK * s:RANK * (s + 1)]

        @pl.loop(0, SLOTS - 1)
        def _(k):
            to = mate(k)
            copy(z_out.at[w, to], z_in.at[w], z_snd.at[w], z_rcv.at[w], 2 * to + core, c).start()

        z_in[w] = z_out[w, 0]

    @pl.when(owner)
    def _():
        local(f_rows.at[pl.ds(1, SLOTS - 1)], f_rcv).wait()
        for s in range(0, SLOTS, 2):
            at = slice(RANK * s, RANK * (s + 2))
            hi, lo = split(jnp.concatenate([poly * f_rows[s], poly * f_rows[s + 1]], axis=0))
            fm_hi[at, :] = hi
            fm_lo[at, :] = lo
        project(0, (l_hi[...], l_lo[...]))
        l_copy.wait_recv()
        for b in range(VB):
            hi, lo = split(l_other[pl.ds(b, NQ, stride=VB), :])
            lx_hi[:, LANES * b:LANES * (b + 1)] = hi
            lx_lo[:, LANES * b:LANES * (b + 1)] = lo
        project(1, (lx_hi[...], lx_lo[...]))

    take_amps(0)
    t_swap.wait_recv()
    take_amps(1)

    amps_re = (rhs_hi[0:O, :], rhs_lo[0:O, :])
    amps_im = (rhs_hi[O:2 * O, :], rhs_lo[O:2 * O, :])
    tf = dot3(f_all, (rhs_hi[...], rhs_lo[...]), NT)
    tx = jnp.concatenate([tf[8:16, 0:O] - tf[16:24, O:], tf[8:16, O:] + tf[16:24, 0:O]], axis=0)
    oo_own = (oo_hi[...], oo_lo[...])
    x_terms = x_left[...] - dot3(split(tx), oo_own, NN)
    x_out[0] = x_terms[0:RANK]
    x_out[1] = x_terms[RANK:]
    x_swap = copy(x_out.at[1 - core], x_in, xp_snd, xp_rcv, peer, c)
    x_swap.start()

    e_win = [flat[half * h + EPS_AT:half * h + EPS_AT + 1, 0:1] for h in range(WIN)]
    vir_rows = e_vir + by_row(VIR_NODES, V)
    w_vir = [weight(vir_rows - (e_win[h] + e_own)) for h in range(WIN)]

    x_swap.wait_recv()
    x_sum[...] = x_out[core] + x_in[...]
    x_copy = copy(x_sum, x_all.at[slot], x_snd, x_rcv, core, c)

    @pl.when(jnp.logical_not(owner))
    def _():
        x_copy.start()

    local(chunks_in, oa_rcv).wait()
    oo_swap = copy(oo_g.at[0], oo_g.at[1], op_snd, op_rcv, peer, c)
    oo_swap.start()

    def occ_of(h):
        return jnp.concatenate([oo_g[h, O * q:O * (q + 1), :] for q in range(QUARTERS)], axis=1)

    tz = jnp.concatenate([tf[0:8, 0:O], tf[0:8, O:]], axis=0)
    tz_turned = jnp.concatenate([tz[:, O // 2:], tz[:, :O // 2]], axis=1)
    dress = [dot3(split(tz), split(occ_of(0)), NN)]
    oo_swap.wait_recv()
    dress.append(dot3(split(tz_turned), split(occ_of(1)), NN))

    def through(ct, slab, occ):
        ct = split(ct)
        lv = dot3(ct, slab, NN)
        r = split(dot3(ct, occ, NT))
        rt_re, rt_im = dot3(r, amps_re, NN), dot3(r, amps_im, NN)
        parts = []
        for g in range(0, lv.shape[0], 16):
            re, im = slice(g, g + 8), slice(g + 8, g + 16)
            parts.append((
                lv[re] - (rt_re[re] - rt_im[im]),
                lv[im] - (rt_im[re] + rt_re[im]),
            ))
        return parts

    @pl.when(jnp.logical_not(owner))
    def _():
        for w in range(WIN):
            local(z_in.at[w], z_rcv.at[w]).wait()

    cols = jnp.concatenate(
        [part for h in range(WIN) for part in (z_in[h] - dress[h][0:8], -dress[h][8:16])], axis=0)
    for h, v in enumerate(through(cols, (l_hi[...], l_lo[...]), oo_own)):
        re, im = fold(w_vir[h], v)
        om[h, :, 0:V] = -re
        om[h, :, V:2 * V] = -im
    first = copy(om.at[1], om_in, r1_snd, r1_rcv, peer, c)
    first.start()

    @pl.when(owner)
    def _():
        local(x_all.at[pl.ds(1, SLOTS - 1)], x_rcv).wait()
        total = x_sum[...]
        for k in range(1, SLOTS):
            total = total + x_all[k]
        x_tot[core] = total
        swap = copy(x_tot.at[core], x_tot.at[core], xs_snd, xs_rcv, peer, c)
        swap.start()
        w_re, w_im = weight(e_vir + by_row(PAIR_NODES, V) - e_win[0])
        turns = [HALF * (g - PAIR_MID) for g in PAIR_NODES]
        t_cos = by_row([math.cos(g) for g in turns], V)
        t_sin = by_row([math.sin(g) for g in turns], V)
        local(x_tot.at[1 - core], xs_rcv).wait()
        v, = through(jnp.concatenate([x_tot[0], x_tot[1]], axis=0), (l_hi[...], l_lo[...]), oo_own)
        re, im = fold((w_re * t_cos - w_im * t_sin, w_re * t_sin + w_im * t_cos), v)
        om[0, :, 0:V] += 2.0 * re
        om[0, :, V:2 * V] += 2.0 * im
        swap.wait_send()

    first.wait_recv()
    om_pl[plane] = om[0] + om_in[...]

    @pl.loop(PLANE, SLOTS - 1)
    def _(k):
        copy(om_pl.at[plane], om_pl.at[plane], r2_snd, r2_rcv, 2 * mate(k) + core, c).start()

    local(om_pl.at[pl.ds(0, PLANE - 1)], r2_rcv).wait()
    total = om_pl[0]
    for k in range(1, PLANE):
        total = total + om_pl[k]
    om_ln[line] = total
    for k in far_line:
        pair, chol = line_mate(k)
        copy(om_ln.at[line], om_ln.at[line], r3_snd, r3_rcv, pair, chol).start()
    local(om_ln.at[pl.ds(0, LINE - 1)], r3_rcv).wait()
    total = om_ln[0]
    for k in range(1, LINE):
        total = total + om_ln[k]
    om_fin[core] = total
    last = copy(om_fin.at[core], om_fin.at[core], r4_snd, r4_rcv, peer, c)
    last.start()
    last_in = om_fin.at[1 - core]
    local(last_in, r4_rcv).wait()
    for i in range(WIN):
        for r in range(2):
            out[r, i:i + 1, :] = om_fin[i, :, r * V:(r + 1) * V]

    last.wait_send()
    local(om_ln.at[pl.ds(0, LINE - 1)], r3_snd).wait()
    local(om_pl.at[pl.ds(0, PLANE - 1)], r2_snd).wait()
    first.wait_send()
    x_swap.wait_send()
    t_swap.wait_send()
    oo_swap.wait_send()
    local(msg.at[pl.ds(0, SLOTS - 1), pl.ds(0, SENT)], t_snd).wait()
    local(chunks_in, oa_snd).wait()

    @pl.when(jnp.logical_not(owner))
    def _():
        f_copy.wait_send()
        x_copy.wait_send()

    @pl.when(owner)
    def _():
        l_copy.wait_send()
        local(chunks_in, oc_snd).wait()
        for w in range(WIN):
            local(z_out.at[w, pl.ds(0, SLOTS - 1)], z_snd.at[w]).wait()


def per_device(chol_ov, chol_oo, amplitudes, eps_occ, eps_vir, fock):
    dma = pltpu.SemaphoreType.DMA

    def f32(*shape):
        return pltpu.VMEM(shape, F32)

    def b16(*shape):
        return pltpu.VMEM(shape, BF16)

    scratch = [
        f32(NQ * VB, LANES), f32(O, NQ), f32(2, 1, V), pltpu.SMEM((1,), F32), f32(V), f32(1, V), dma((6,)),
        f32(O * QUARTERS, LANES), f32(O * QUARTERS, LANES), b16(O, NQ), b16(O, NQ),
        b16(NQ, V), b16(NQ, V), f32(2 * RANK, NQ), f32(PAIR, MSG, LANES),
        f32(SLOTS, 1, V), f32(NQ * VB, LANES), b16(NQ, V), b16(NQ, V), f32(WIN, O * QUARTERS, LANES),
        b16(RANK * SLOTS, V), b16(RANK * SLOTS, V), b16(2 * O, V), b16(2 * O, V),
        f32(WIN, SLOTS, RANK, NQ), f32(WIN, RANK, NQ),
        f32(2, RANK, NQ), f32(RANK, NQ), f32(RANK, NQ), f32(SLOTS, RANK, NQ), f32(2, RANK, NQ),
        f32(WIN, 1, 2 * V), f32(1, 2 * V), f32(PLANE, 1, 2 * V), f32(LINE, 1, 2 * V), f32(WIN, 1, 2 * V),
        dma((WIN,)), dma((WIN,)),
    ] + [dma] * 28
    hbm = pl.BlockSpec(memory_space=pltpu.HBM)
    return pl.pallas_call(
        kernel,
        out_shape=jax.ShapeDtypeStruct((2, WIN, V), F32),
        in_specs=[hbm] * 6,
        out_specs=pl.BlockSpec(memory_space=pltpu.VMEM),
        scratch_shapes=scratch,
        compiler_params=pltpu.CompilerParams(
            collective_id=0, has_side_effects=True, vmem_limit_bytes=63 * 2**20
        ),
    )(
        chol_ov.reshape(NQ * VB, LANES), chol_oo.reshape(NQ, O).T, amplitudes, eps_occ, eps_vir, fock
    )


def solution(mesh):
    return jax.shard_map(
        per_device,
        mesh=mesh,
        in_specs=(
            P("chol", "pair", None),
            P("chol", "pair", None),
            P(None, "pair", None),
            P("pair"),
            P(),
            P("pair", None),
        ),
        out_specs=P(),
        check_vma=False,
    )
```

time: 47.8 us -> 44.7 us (0.935)
  local copies, waits for them, and re-layouts: 4.54 us -> 1.31 us
    unnamed x6 -> x1, local copies, waits for them, and re-layouts: 3.85 us -> 1.31 us
    reshape x1 -> x0, local copies, waits for them, and re-layouts: 0.69 us -> none  [per_device(): eps_vir.reshape(1, V)]
where the time goes in v2:
time: 44.7 us; the launch traced here: 44.5 us
  Pallas kernels  42.5 us (95%)
  local copies, waits for them, and re-layouts  1.31 us (3%)
  between operations  0.66 us (1%)
    pallas_call x1, Pallas kernels, per_device(): pl.pallas_call(kernel, out_shape=jax.ShapeDtypeStruct((2, WIN, V), F32),...  42.5 us
    unnamed x1, local copies, waits for them, and re-layouts  1.31 us

profile of v2, /device:TPU:1, one launch (start us, length us, event | category | flops | bytes accessed | tf_op | source)
XLA Modules:
  0.0 44.5 jit_solution(1584225438936291360)
XLA Ops:
  0.7 42.5 %shard_map.64 = f32[2,2,768]{2,1,0:T(2,128)} custom-call(f32[3072,128]{1,0:T(8,128)} %bitcast.4, f32[64,512]{1,0:T(8,128)} %bitcast.5, f32[2,1,768]{2,1,0:T(1,128)} %amps.1, f32[1]{0:T(128)S(6)} %copy.8.eocc, f32[768]{0:T(1024)} %evir.1, f32[1,768]{1,0:T(1,128)} %fock.1), custom_call_target="tpu_custom_call" | custom-call | tf_op jit(solution)/shard_map/pallas_call | solution.py:452
  43.2 1.3 %copy.9 = f32[2,2,768]{2,1,0:T(2,128)} copy(f32[2,2,768]{2,1,0:T(2,128)} %shard_map.64) | data formatting | bytes 24576

commit v3 on v2

--- a/solution.py
+++ b/solution.py
@@ -93,6 +93,17 @@
     return both[:rows] + both[rows:] + dot(a_hi, b_lo, dims)
 
 
+RING = (0, 1, 2, 1)
+DIRECT = sorted(
+    (at for at in range(1, SLOTS) if at < PLANE or at % 2 == 0),
+    key=lambda at: -(at // PLANE + RING[at // 4 % 4] + RING[at % 4]),
+)
+
+
+def held_at(at):
+    return at if at < PLANE else PLANE + 4 * (at % 4) + (at - PLANE) // 4
+
+
 def far_first(v):
     return 2 + v - (v // 2) * (2 * v - 1)
 
@@ -101,9 +112,9 @@
     ov, oo, amps, eocc, evir, fock, out,
     raw, oo_in, amps_in, e_in, ev_in, f_in, in_sem,
     oo_q, oo_p, oo_hi, oo_lo, l_hi, l_lo, x_left, msg,
-    f_rows, l_other, lx_hi, lx_lo, oo_g, fm_hi, fm_lo, rhs_hi, rhs_lo, z_out, z_in,
-    x_out, x_in, x_sum, x_all, x_tot, om, om_in, om_pl, om_ln, om_fin,
-    z_snd, z_rcv, l_snd, l_rcv, f_snd, f_rcv, x_snd, x_rcv, xs_snd, xs_rcv, t_snd, t_rcv, tp_snd, tp_rcv,
+    f_rows, l_other, lx_hi, lx_lo, oo_g, fm_hi, fm_lo, rhs_hi, rhs_lo, z_out, z_in, z_held,
+    x_out, x_in, x_sum, x_row, x_head, x_all, x_tot, om, om_in, om_pl, om_ln, om_fin,
+    z_snd, z_rcv, zh_rcv, zh_snd, xr_rcv, xh_snd, l_snd, l_rcv, f_snd, f_rcv, x_snd, x_rcv, xs_snd, xs_rcv, t_snd, t_rcv, tp_snd, tp_rcv,
     oc_snd, oc_rcv, oa_snd, oa_rcv, op_snd, op_rcv, xp_snd, xp_rcv, r1_snd, r1_rcv, r2_snd, r2_rcv, r3_snd, r3_rcv, r4_snd, r4_rcv,
 ):
     p, c = lax.axis_index("pair"), lax.axis_index("chol")
@@ -135,6 +146,8 @@
 
     far_line = (4, 3, 5, 2, 6, 1, 7)
     owner = slot == 0
+    head = slot < 4
+    relay = (slot == 1) | (slot == 3)
 
     inputs = [
         pltpu.make_async_copy(src, dst, in_sem.at[i])
@@ -264,13 +277,12 @@
     def project(w, slab):
         z = dot3((fm_hi[...], fm_lo[...]), slab, NT)
         for s in range(SLOTS):
-            z_out[w, s] = z[RANK * s:RANK * (s + 1)]
-
-        @pl.loop(0, SLOTS - 1)
-        def _(k):
-            to = mate(k)
-            copy(z_out.at[w, to], z_in.at[w], z_snd.at[w], z_rcv.at[w], 2 * to + core, c).start()
-
+            z_out[w, held_at(s)] = z[RANK * s:RANK * (s + 1)]
+        for y in (1, 3):
+            block = z_out.at[w, pl.ds(PLANE + 4 * y, 4)]
+            copy(block, z_held.at[w], z_snd.at[w], zh_rcv.at[w], 2 * y + core, c).start()
+        for to in DIRECT:
+            copy(z_out.at[w, held_at(to)], z_in.at[w], z_snd.at[w], z_rcv.at[w], 2 * to + core, c).start()
         z_in[w] = z_out[w, 0]
 
     @pl.when(owner)
@@ -310,11 +322,31 @@
 
     x_swap.wait_recv()
     x_sum[...] = x_out[core] + x_in[...]
-    x_copy = copy(x_sum, x_all.at[slot], x_snd, x_rcv, core, c)
-
-    @pl.when(jnp.logical_not(owner))
+    x_copy = copy(x_sum, x_row.at[slot // 4], x_snd, xr_rcv, 2 * y_at + core, c)
+    head_copy = copy(x_head, x_all.at[slot], xh_snd, x_rcv, core, c)
+
+    @pl.when(jnp.logical_not(head))
     def _():
         x_copy.start()
+
+    @pl.when(relay)
+    def _():
+        for w in range(WIN):
+            local(z_held.at[w], zh_rcv.at[w]).wait()
+            for x in range(4):
+                copy(z_held.at[w, x], z_in.at[w], zh_snd, z_rcv.at[w], 2 * (PLANE + 4 * x) + p, c).start()
+
+    @pl.when(head)
+    def _():
+        local(x_row.at[pl.ds(1, 7)], xr_rcv).wait()
+        total = x_sum[...]
+        for k in range(1, 8):
+            total = total + x_row[k]
+        x_head[...] = total
+
+        @pl.when(jnp.logical_not(owner))
+        def _():
+            head_copy.start()
 
     local(chunks_in, oa_rcv).wait()
     oo_swap = copy(oo_g.at[0], oo_g.at[1], op_snd, op_rcv, peer, c)
@@ -359,11 +391,8 @@
 
     @pl.when(owner)
     def _():
-        local(x_all.at[pl.ds(1, SLOTS - 1)], x_rcv).wait()
-        total = x_sum[...]
-        for k in range(1, SLOTS):
-            total = total + x_all[k]
-        x_tot[core] = total
+        local(x_all.at[pl.ds(1, 3)], x_rcv).wait()
+        x_tot[core] = x_head[...] + x_all[1] + x_all[2] + x_all[3]
         swap = copy(x_tot.at[core], x_tot.at[core], xs_snd, xs_rcv, peer, c)
         swap.start()
         w_re, w_im = weight(e_vir + by_row(PAIR_NODES, V) - e_win[0])
@@ -418,7 +447,18 @@
     @pl.when(jnp.logical_not(owner))
     def _():
         f_copy.wait_send()
+
+    @pl.when(jnp.logical_not(head))
+    def _():
         x_copy.wait_send()
+
+    @pl.when(head & jnp.logical_not(owner))
+    def _():
+        head_copy.wait_send()
+
+    @pl.when(relay)
+    def _():
+        local(z_held, zh_snd).wait()
 
     @pl.when(owner)
     def _():
@@ -443,11 +483,12 @@
         b16(NQ, V), b16(NQ, V), f32(2 * RANK, NQ), f32(PAIR, MSG, LANES),
         f32(SLOTS, 1, V), f32(NQ * VB, LANES), b16(NQ, V), b16(NQ, V), f32(WIN, O * QUARTERS, LANES),
         b16(RANK * SLOTS, V), b16(RANK * SLOTS, V), b16(2 * O, V), b16(2 * O, V),
-        f32(WIN, SLOTS, RANK, NQ), f32(WIN, RANK, NQ),
-        f32(2, RANK, NQ), f32(RANK, NQ), f32(RANK, NQ), f32(SLOTS, RANK, NQ), f32(2, RANK, NQ),
+        f32(WIN, SLOTS, RANK, NQ), f32(WIN, RANK, NQ), f32(WIN, 4, RANK, NQ),
+        f32(2, RANK, NQ), f32(RANK, NQ), f32(RANK, NQ), f32(8, RANK, NQ), f32(RANK, NQ),
+        f32(4, RANK, NQ), f32(2, RANK, NQ),
         f32(WIN, 1, 2 * V), f32(1, 2 * V), f32(PLANE, 1, 2 * V), f32(LINE, 1, 2 * V), f32(WIN, 1, 2 * V),
-        dma((WIN,)), dma((WIN,)),
-    ] + [dma] * 28
+        dma((WIN,)), dma((WIN,)), dma((WIN,)),
+    ] + [dma] * 31
     hbm = pl.BlockSpec(memory_space=pltpu.HBM)
     return pl.pallas_call(
         kernel,

time: 44.7 us -> 42.9 us (0.960)
  Pallas kernels: 42.5 us -> 40.7 us
    pallas_call x1, Pallas kernels: 42.5 us -> 40.7 us  [per_device(): pl.pallas_call(kernel, out_shape=jax.ShapeDtypeStruct((2, WIN, V), F32),...]
where the time goes in v3:
time: 42.9 us; the launch traced here: 42.7 us
  Pallas kernels  40.7 us (95%)
  local copies, waits for them, and re-layouts  1.31 us (3%)
  between operations  0.66 us (2%)
    pallas_call x1, Pallas kernels, per_device(): pl.pallas_call(kernel, out_shape=jax.ShapeDtypeStruct((2, WIN, V), F32),...  40.7 us
    unnamed x1, local copies, waits for them, and re-layouts  1.31 us

profile of v3, /device:TPU:1, one launch (start us, length us, event | category | flops | bytes accessed | tf_op | source)
XLA Modules:
  0.0 42.7 jit_solution(11474004122877746140)
XLA Ops:
  0.7 40.7 %shard_map.64 = f32[2,2,768]{2,1,0:T(2,128)} custom-call(f32[3072,128]{1,0:T(8,128)} %bitcast.4, f32[64,512]{1,0:T(8,128)} %bitcast.5, f32[2,1,768]{2,1,0:T(1,128)} %amps.1, f32[1]{0:T(128)S(6)} %copy.8.eocc, f32[768]{0:T(1024)} %evir.1, f32[1,768]{1,0:T(1,128)} %fock.1), custom_call_target="tpu_custom_call" | custom-call | tf_op jit(solution)/shard_map/pallas_call | solution.py:493
  41.4 1.3 %copy.9 = f32[2,2,768]{2,1,0:T(2,128)} copy(f32[2,2,768]{2,1,0:T(2,128)} %shard_map.64) | data formatting | bytes 24576

commit v4 on v3

--- a/solution.py
+++ b/solution.py
@@ -112,7 +112,7 @@
     ov, oo, amps, eocc, evir, fock, out,
     raw, oo_in, amps_in, e_in, ev_in, f_in, in_sem,
     oo_q, oo_p, oo_hi, oo_lo, l_hi, l_lo, x_left, msg,
-    f_rows, l_other, lx_hi, lx_lo, oo_g, fm_hi, fm_lo, rhs_hi, rhs_lo, z_out, z_in, z_held,
+    parcel_out, parcel, f_rows, l_other, lx_hi, lx_lo, oo_g, fm_hi, fm_lo, rhs_hi, rhs_lo, z_out, z_in, z_held,
     x_out, x_in, x_sum, x_row, x_head, x_all, x_tot, om, om_in, om_pl, om_ln, om_fin,
     z_snd, z_rcv, zh_rcv, zh_snd, xr_rcv, xh_snd, l_snd, l_rcv, f_snd, f_rcv, x_snd, x_rcv, xs_snd, xs_rcv, t_snd, t_rcv, tp_snd, tp_rcv,
     oc_snd, oc_rcv, oa_snd, oa_rcv, op_snd, op_rcv, xp_snd, xp_rcv, r1_snd, r1_rcv, r2_snd, r2_rcv, r3_snd, r3_rcv, r4_snd, r4_rcv,
@@ -163,16 +163,16 @@
     def greet(pair, chol):
         pl.semaphore_signal(barrier, inc=1, device_id=(pair, chol), device_id_type=MESH)
 
+    @pl.loop(0, SLOTS - 1)
+    def _(k):
+        greet(2 * mate(k) + core, c)
+
+    greet(peer, c)
+
     for k in far_line:
         @pl.when(lax.rem(line + k, LINE) // 2 != c)
         def _(k=k):
             greet(*line_mate(k))
-
-    @pl.loop(0, SLOTS - 1)
-    def _(k):
-        greet(2 * mate(k) + core, c)
-
-    greet(peer, c)
 
     for cp in inputs[:3]:
         cp.wait()
@@ -204,6 +204,13 @@
         oo_hi[:, LANES * q:LANES * (q + 1)] = hi
         oo_lo[:, LANES * q:LANES * (q + 1)] = lo
 
+    @pl.when(owner)
+    def _():
+        for to in range(1, SLOTS):
+            at = O * (to % 4) + 8 * (to // 4)
+            parcel_out[to, 0:8] = oo_p[at:at + 8, :]
+            parcel_out[to, 8:8 + MSG] = msg[0]
+
     inputs[5].wait()
     for b in range(VB):
         hi, lo = split(raw[pl.ds(b, NQ, stride=VB), :])
@@ -228,38 +235,45 @@
         l_copy.start()
         f_rows[0] = f_in[...]
 
-    @pl.loop(0, SLOTS - 1)
-    def _(k):
-        mine = msg.at[slot, pl.ds(0, SENT)]
-        copy(mine, mine, t_snd, t_rcv, 2 * mate(k) + core, c).start()
-
-    def chunk(ref, s):
-        return ref.at[pl.ds(pl.multiple_of(O * lax.rem(s, 4) + 8 * (s // 4), 8), 8)]
-
-    def pass_on():
+    @pl.when(jnp.logical_not(owner))
+    def _():
         @pl.loop(0, SLOTS - 1)
         def _(k):
-            mine = chunk(oo_own_w, slot)
-            copy(mine, mine, oa_snd, oa_rcv, 2 * mate(k) + core, c).start()
-
-    oo_own_w = oo_g.at[0]
-
-    @pl.when(owner)
-    def _():
+            mine = msg.at[slot, pl.ds(0, SENT)]
+            copy(mine, mine, t_snd, t_rcv, 2 * mate(k) + core, c).start()
+
+    def pass_on(mine, into):
         @pl.loop(0, SLOTS - 1)
         def _(k):
-            to = mate(k)
-            copy(chunk(oo_p, to), chunk(oo_own_w, to), oc_snd, oc_rcv, 2 * to + core, c).start()
+            copy(mine, into, oa_snd, oa_rcv, 2 * mate(k) + core, c).start()
+
+    oo_own_w = oo_g.at[0]
+
+    def own_chunk(at):
+        return oo_own_w.at[pl.ds(at, 8)]
+
+    @pl.when(owner)
+    def _():
+        for to in sorted(range(1, SLOTS), key=lambda at: -(at // PLANE + RING[at // 4 % 4] + RING[at % 4])):
+            copy(parcel_out.at[to], parcel, oc_snd, oc_rcv, 2 * to + core, c).start()
 
         oo_g[0, 0:8, :] = oo_p[0:8, :]
-        pass_on()
+        pass_on(own_chunk(0), own_chunk(0))
 
     half = MSG * SLOTS
     chunks_in = oo_p.at[pl.ds(0, 8 * (SLOTS - 1))]
-    local(msg.at[pl.ds(0, SLOTS - 1), pl.ds(0, SENT)], t_rcv).wait()
+    @pl.when(jnp.logical_not(owner))
+    def _():
+        local(msg.at[pl.ds(0, SLOTS - 2), pl.ds(0, SENT)], t_rcv).wait()
+        local(parcel, oc_rcv).wait()
+        msg[0] = parcel[8:8 + MSG]
+
     t_swap = copy(msg.at[pl.ds(0, SLOTS), pl.ds(0, SENT)], msg.at[pl.ds(SLOTS, SLOTS), pl.ds(0, SENT)],
                   tp_snd, tp_rcv, peer, c)
-    t_swap.start()
+
+    @pl.when(jnp.logical_not(owner))
+    def _():
+        t_swap.start()
 
     def take_amps(h):
         for r in range(2):
@@ -271,8 +285,9 @@
 
     @pl.when(jnp.logical_not(owner))
     def _():
-        local(chunk(oo_own_w, slot), oc_rcv).wait()
-        pass_on()
+        at = pl.multiple_of(O * lax.rem(slot, 4) + 8 * (slot // 4), 8)
+        oo_g[0, pl.ds(at, 8), :] = parcel[0:8]
+        pass_on(parcel.at[pl.ds(0, 8)], own_chunk(at))
 
     def project(w, slab):
         z = dot3((fm_hi[...], fm_lo[...]), slab, NT)
@@ -287,6 +302,11 @@
 
     @pl.when(owner)
     def _():
+        l_copy.wait_recv()
+        for b in range(VB):
+            hi, lo = split(l_other[pl.ds(b, NQ, stride=VB), :])
+            lx_hi[:, LANES * b:LANES * (b + 1)] = hi
+            lx_lo[:, LANES * b:LANES * (b + 1)] = lo
         local(f_rows.at[pl.ds(1, SLOTS - 1)], f_rcv).wait()
         for s in range(0, SLOTS, 2):
             at = slice(RANK * s, RANK * (s + 2))
@@ -294,11 +314,8 @@
             fm_hi[at, :] = hi
             fm_lo[at, :] = lo
         project(0, (l_hi[...], l_lo[...]))
-        l_copy.wait_recv()
-        for b in range(VB):
-            hi, lo = split(l_other[pl.ds(b, NQ, stride=VB), :])
-            lx_hi[:, LANES * b:LANES * (b + 1)] = hi
-            lx_lo[:, LANES * b:LANES * (b + 1)] = lo
+        local(msg.at[pl.ds(0, SLOTS - 1), pl.ds(0, SENT)], t_rcv).wait()
+        t_swap.start()
         project(1, (lx_hi[...], lx_lo[...]))
 
     take_amps(0)
@@ -320,6 +337,13 @@
     vir_rows = e_vir + by_row(VIR_NODES, V)
     w_vir = [weight(vir_rows - (e_win[h] + e_own)) for h in range(WIN)]
 
+    @pl.when(relay)
+    def _():
+        for w in (0,):
+            local(z_held.at[w], zh_rcv.at[w]).wait()
+            for x in range(4):
+                copy(z_held.at[w, x], z_in.at[w], zh_snd, z_rcv.at[w], 2 * (PLANE + 4 * x) + p, c).start()
+
     x_swap.wait_recv()
     x_sum[...] = x_out[core] + x_in[...]
     x_copy = copy(x_sum, x_row.at[slot // 4], x_snd, xr_rcv, 2 * y_at + core, c)
@@ -331,7 +355,7 @@
 
     @pl.when(relay)
     def _():
-        for w in range(WIN):
+        for w in (1,):
             local(z_held.at[w], zh_rcv.at[w]).wait()
             for x in range(4):
                 copy(z_held.at[w, x], z_in.at[w], zh_snd, z_rcv.at[w], 2 * (PLANE + 4 * x) + p, c).start()
@@ -382,12 +406,20 @@
 
     cols = jnp.concatenate(
         [part for h in range(WIN) for part in (z_in[h] - dress[h][0:8], -dress[h][8:16])], axis=0)
-    for h, v in enumerate(through(cols, (l_hi[...], l_lo[...]), oo_own)):
-        re, im = fold(w_vir[h], v)
-        om[h, :, 0:V] = -re
-        om[h, :, V:2 * V] = -im
+    slab = (l_hi[...], l_lo[...])
+
+    def exchange(parts):
+        for h in range(WIN):
+            re, im = fold(w_vir[h], parts[h])
+            om[h, :, 0:V] = -re
+            om[h, :, V:2 * V] = -im
+
     first = copy(om.at[1], om_in, r1_snd, r1_rcv, peer, c)
-    first.start()
+
+    @pl.when(jnp.logical_not(owner))
+    def _():
+        exchange(through(cols, slab, oo_own))
+        first.start()
 
     @pl.when(owner)
     def _():
@@ -400,8 +432,10 @@
         t_cos = by_row([math.cos(g) for g in turns], V)
         t_sin = by_row([math.sin(g) for g in turns], V)
         local(x_tot.at[1 - core], xs_rcv).wait()
-        v, = through(jnp.concatenate([x_tot[0], x_tot[1]], axis=0), (l_hi[...], l_lo[...]), oo_own)
-        re, im = fold((w_re * t_cos - w_im * t_sin, w_re * t_sin + w_im * t_cos), v)
+        parts = through(jnp.concatenate([cols, x_tot[0], x_tot[1]], axis=0), slab, oo_own)
+        exchange(parts)
+        first.start()
+        re, im = fold((w_re * t_cos - w_im * t_sin, w_re * t_sin + w_im * t_cos), parts[WIN])
         om[0, :, 0:V] += 2.0 * re
         om[0, :, V:2 * V] += 2.0 * im
         swap.wait_send()
@@ -441,12 +475,12 @@
     x_swap.wait_send()
     t_swap.wait_send()
     oo_swap.wait_send()
-    local(msg.at[pl.ds(0, SLOTS - 1), pl.ds(0, SENT)], t_snd).wait()
     local(chunks_in, oa_snd).wait()
 
     @pl.when(jnp.logical_not(owner))
     def _():
         f_copy.wait_send()
+        local(msg.at[pl.ds(0, SLOTS - 1), pl.ds(0, SENT)], t_snd).wait()
 
     @pl.when(jnp.logical_not(head))
     def _():
@@ -463,7 +497,7 @@
     @pl.when(owner)
     def _():
         l_copy.wait_send()
-        local(chunks_in, oc_snd).wait()
+        local(parcel_out.at[pl.ds(1, SLOTS - 1)], oc_snd).wait()
         for w in range(WIN):
             local(z_out.at[w, pl.ds(0, SLOTS - 1)], z_snd.at[w]).wait()
 
@@ -481,7 +515,7 @@
         f32(NQ * VB, LANES), f32(O, NQ), f32(2, 1, V), pltpu.SMEM((1,), F32), f32(V), f32(1, V), dma((6,)),
         f32(O * QUARTERS, LANES), f32(O * QUARTERS, LANES), b16(O, NQ), b16(O, NQ),
         b16(NQ, V), b16(NQ, V), f32(2 * RANK, NQ), f32(PAIR, MSG, LANES),
-        f32(SLOTS, 1, V), f32(NQ * VB, LANES), b16(NQ, V), b16(NQ, V), f32(WIN, O * QUARTERS, LANES),
+        f32(SLOTS, 8 + MSG, LANES), f32(8 + MSG, LANES), f32(SLOTS, 1, V), f32(NQ * VB, LANES), b16(NQ, V), b16(NQ, V), f32(WIN, O * QUARTERS, LANES),
         b16(RANK * SLOTS, V), b16(RANK * SLOTS, V), b16(2 * O, V), b16(2 * O, V),
         f32(WIN, SLOTS, RANK, NQ), f32(WIN, RANK, NQ), f32(WIN, 4, RANK, NQ),
         f32(2, RANK, NQ), f32(RANK, NQ), f32(RANK, NQ), f32(8, RANK, NQ), f32(RANK, NQ),

time: 42.9 us -> 42.5 us (level)
  no operation moved by 1% of the time
where the time goes in v4:
time: 42.5 us; the launch traced here: 42.3 us
  Pallas kernels  40.3 us (95%)
  local copies, waits for them, and re-layouts  1.31 us (3%)
  between operations  0.66 us (2%)
    pallas_call x1, Pallas kernels, per_device(): pl.pallas_call(kernel, out_shape=jax.ShapeDtypeStruct((2, WIN, V), F32),...  40.3 us
    unnamed x1, local copies, waits for them, and re-layouts  1.31 us

profile of v4, /device:TPU:1, one launch (start us, length us, event | category | flops | bytes accessed | tf_op | source)
XLA Modules:
  0.0 42.3 jit_solution(2118697906909443855)
XLA Ops:
  0.7 40.3 %shard_map.64 = f32[2,2,768]{2,1,0:T(2,128)} custom-call(f32[3072,128]{1,0:T(8,128)} %bitcast.4, f32[64,512]{1,0:T(8,128)} %bitcast.5, f32[2,1,768]{2,1,0:T(1,128)} %amps.1, f32[1]{0:T(128)S(6)} %copy.8.eocc, f32[768]{0:T(1024)} %evir.1, f32[1,768]{1,0:T(1,128)} %fock.1), custom_call_target="tpu_custom_call" | custom-call | tf_op jit(solution)/shard_map/pallas_call | solution.py:527
  41.0 1.3 %copy.9 = f32[2,2,768]{2,1,0:T(2,128)} copy(f32[2,2,768]{2,1,0:T(2,128)} %shard_map.64) | data formatting | bytes 24576

commit v5 on v4

--- a/solution.py
+++ b/solution.py
@@ -408,18 +408,19 @@
         [part for h in range(WIN) for part in (z_in[h] - dress[h][0:8], -dress[h][8:16])], axis=0)
     slab = (l_hi[...], l_lo[...])
 
+    first = copy(om.at[1], om_in, r1_snd, r1_rcv, peer, c)
+
     def exchange(parts):
-        for h in range(WIN):
+        for h in (1, 0):
             re, im = fold(w_vir[h], parts[h])
             om[h, :, 0:V] = -re
             om[h, :, V:2 * V] = -im
-
-    first = copy(om.at[1], om_in, r1_snd, r1_rcv, peer, c)
+            if h:
+                first.start()
 
     @pl.when(jnp.logical_not(owner))
     def _():
         exchange(through(cols, slab, oo_own))
-        first.start()
 
     @pl.when(owner)
     def _():
@@ -434,7 +435,6 @@
         local(x_tot.at[1 - core], xs_rcv).wait()
         parts = through(jnp.concatenate([cols, x_tot[0], x_tot[1]], axis=0), slab, oo_own)
         exchange(parts)
-        first.start()
         re, im = fold((w_re * t_cos - w_im * t_sin, w_re * t_sin + w_im * t_cos), parts[WIN])
         om[0, :, 0:V] += 2.0 * re
         om[0, :, V:2 * V] += 2.0 * im

time: 42.5 us -> 42.5 us (level)
  no operation moved by 1% of the time
where the time goes in v5:
time: 42.5 us; the launch traced here: 42.3 us
  Pallas kernels  40.3 us (95%)
  local copies, waits for them, and re-layouts  1.31 us (3%)
  between operations  0.66 us (2%)
    pallas_call x1, Pallas kernels, per_device(): pl.pallas_call(kernel, out_shape=jax.ShapeDtypeStruct((2, WIN, V), F32),...  40.3 us
    unnamed x1, local copies, waits for them, and re-layouts  1.31 us

profile of v5, /device:TPU:1, one launch (start us, length us, event | category | flops | bytes accessed | tf_op | source)
XLA Modules:
  0.0 42.3 jit_solution(13118497492462711268)
XLA Ops:
  0.7 40.3 %shard_map.64 = f32[2,2,768]{2,1,0:T(2,128)} custom-call(f32[3072,128]{1,0:T(8,128)} %bitcast.4, f32[64,512]{1,0:T(8,128)} %bitcast.5, f32[2,1,768]{2,1,0:T(1,128)} %amps.1, f32[1]{0:T(128)S(6)} %copy.8.eocc, f32[768]{0:T(1024)} %evir.1, f32[1,768]{1,0:T(1,128)} %fock.1), custom_call_target="tpu_custom_call" | custom-call | tf_op jit(solution)/shard_map/pallas_call | solution.py:527
  41.0 1.3 %copy.9 = f32[2,2,768]{2,1,0:T(2,128)} copy(f32[2,2,768]{2,1,0:T(2,128)} %shard_map.64) | data formatting | bytes 24576

commit v6 on v5

--- a/solution.py
+++ b/solution.py
@@ -113,9 +113,9 @@
     raw, oo_in, amps_in, e_in, ev_in, f_in, in_sem,
     oo_q, oo_p, oo_hi, oo_lo, l_hi, l_lo, x_left, msg,
     parcel_out, parcel, f_rows, l_other, lx_hi, lx_lo, oo_g, fm_hi, fm_lo, rhs_hi, rhs_lo, z_out, z_in, z_held,
-    x_out, x_in, x_sum, x_row, x_head, x_all, x_tot, om, om_in, om_pl, om_ln, om_fin,
+    x_out, x_in, x_sum, x_row, x_head, x_all, x_tot, om, om_in, om_pl, om_ln,
     z_snd, z_rcv, zh_rcv, zh_snd, xr_rcv, xh_snd, l_snd, l_rcv, f_snd, f_rcv, x_snd, x_rcv, xs_snd, xs_rcv, t_snd, t_rcv, tp_snd, tp_rcv,
-    oc_snd, oc_rcv, oa_snd, oa_rcv, op_snd, op_rcv, xp_snd, xp_rcv, r1_snd, r1_rcv, r2_snd, r2_rcv, r3_snd, r3_rcv, r4_snd, r4_rcv,
+    oc_snd, oc_rcv, oa_snd, oa_rcv, op_snd, op_rcv, xp_snd, xp_rcv, r1_snd, r1_rcv, r2_snd, r2_rcv, r3_snd, r3_rcv,
 ):
     p, c = lax.axis_index("pair"), lax.axis_index("chol")
     core = lax.rem(p, 2)
@@ -168,6 +168,9 @@
         greet(2 * mate(k) + core, c)
 
     greet(peer, c)
+    for k in far_line:
+        pair, chol = line_mate(k)
+        greet(pair + peer - p, chol)
 
     for k in far_line:
         @pl.when(lax.rem(line + k, LINE) // 2 != c)
@@ -220,7 +223,7 @@
 
     pl.semaphore_wait(
         barrier,
-        1 + (SLOTS - 1) + (LINE - 2),
+        1 + (SLOTS - 1) + (LINE - 2) + (LINE - 1),
     )
 
     f_copy = copy(f_in, f_rows.at[slot], f_snd, f_rcv, core, c)
@@ -451,25 +454,23 @@
     total = om_pl[0]
     for k in range(1, PLANE):
         total = total + om_pl[k]
-    om_ln[line] = total
+    om_ln[core, line] = total
+    mine = om_ln.at[core, line]
     for k in far_line:
         pair, chol = line_mate(k)
-        copy(om_ln.at[line], om_ln.at[line], r3_snd, r3_rcv, pair, chol).start()
-    local(om_ln.at[pl.ds(0, LINE - 1)], r3_rcv).wait()
-    total = om_ln[0]
-    for k in range(1, LINE):
-        total = total + om_ln[k]
-    om_fin[core] = total
-    last = copy(om_fin.at[core], om_fin.at[core], r4_snd, r4_rcv, peer, c)
-    last.start()
-    last_in = om_fin.at[1 - core]
-    local(last_in, r4_rcv).wait()
+        copy(mine, mine, r3_snd, r3_rcv, pair, chol).start()
+        copy(mine, mine, r3_snd, r3_rcv, pair + peer - p, chol).start()
+    copy(mine, mine, r3_snd, r3_rcv, peer, c).start()
+    lines = om_ln.reshape(2 * LINE, 1, 2 * V).at[pl.ds(0, 2 * LINE - 1)]
+    local(lines, r3_rcv).wait()
     for i in range(WIN):
+        total = om_ln[i, 0]
+        for k in range(1, LINE):
+            total = total + om_ln[i, k]
         for r in range(2):
-            out[r, i:i + 1, :] = om_fin[i, :, r * V:(r + 1) * V]
-
-    last.wait_send()
-    local(om_ln.at[pl.ds(0, LINE - 1)], r3_snd).wait()
+            out[r, i:i + 1, :] = total[:, r * V:(r + 1) * V]
+
+    local(lines, r3_snd).wait()
     local(om_pl.at[pl.ds(0, PLANE - 1)], r2_snd).wait()
     first.wait_send()
     x_swap.wait_send()
@@ -520,9 +521,9 @@
         f32(WIN, SLOTS, RANK, NQ), f32(WIN, RANK, NQ), f32(WIN, 4, RANK, NQ),
         f32(2, RANK, NQ), f32(RANK, NQ), f32(RANK, NQ), f32(8, RANK, NQ), f32(RANK, NQ),
         f32(4, RANK, NQ), f32(2, RANK, NQ),
-        f32(WIN, 1, 2 * V), f32(1, 2 * V), f32(PLANE, 1, 2 * V), f32(LINE, 1, 2 * V), f32(WIN, 1, 2 * V),
+        f32(WIN, 1, 2 * V), f32(1, 2 * V), f32(PLANE, 1, 2 * V), f32(WIN, LINE, 1, 2 * V),
         dma((WIN,)), dma((WIN,)), dma((WIN,)),
-    ] + [dma] * 31
+    ] + [dma] * 29
     hbm = pl.BlockSpec(memory_space=pltpu.HBM)
     return pl.pallas_call(
         kernel,

time: 42.5 us -> 42.1 us (level)
  no operation moved by 1% of the time
where the time goes in v6:
time: 42.1 us; the launch traced here: 42 us
  Pallas kernels  40 us (95%)
  local copies, waits for them, and re-layouts  1.31 us (3%)
  between operations  0.66 us (2%)
    pallas_call x1, Pallas kernels, per_device(): pl.pallas_call(kernel, out_shape=jax.ShapeDtypeStruct((2, WIN, V), F32),...  40 us
    unnamed x1, local copies, waits for them, and re-layouts  1.31 us

profile of v6, /device:TPU:1, one launch (start us, length us, event | category | flops | bytes accessed | tf_op | source)
XLA Modules:
  0.0 42.0 jit_solution(16741169805573758891)
XLA Ops:
  0.7 40.0 %shard_map.64 = f32[2,2,768]{2,1,0:T(2,128)} custom-call(f32[3072,128]{1,0:T(8,128)} %bitcast.4, f32[64,512]{1,0:T(8,128)} %bitcast.5, f32[2,1,768]{2,1,0:T(1,128)} %amps.1, f32[1]{0:T(128)S(6)} %copy.8.eocc, f32[768]{0:T(1024)} %evir.1, f32[1,768]{1,0:T(1,128)} %fock.1), custom_call_target="tpu_custom_call" | custom-call | tf_op jit(solution)/shard_map/pallas_call | solution.py:528
  40.7 1.3 %copy.9 = f32[2,2,768]{2,1,0:T(2,128)} copy(f32[2,2,768]{2,1,0:T(2,128)} %shard_map.64) | data formatting | bytes 24576
